TPU v7x, 32 devices: a whole 2x2x4 slice. The times are simulated.
32 devices in a mesh: narrow: 1, wide: 32 (over z, y, x, core).
Axes of the slice: x: 2, y: 2, z: 4, core: 2. Of those that a mesh axis runs over, the one named last changes fastest.
Arguments:
- pair_act: float32 [256, 256, 128], P('narrow', 'wide'), may hold values from -6 to 6
- block_mask: int32 [4, 4], replicated, may hold values from 0 to 1, as said below
- left_weight: bfloat16 [128, 256], replicated, may hold values from -0.5 to 0.5
- right_weight: bfloat16 [128, 256], replicated, may hold values from -0.5 to 0.5
- gate_weight: bfloat16 [128, 128], replicated, may hold values from -0.5 to 0.5
- out_weight: bfloat16 [128, 128], replicated, may hold values from -0.5 to 0.5
Outputs:
- update: float32 [256, 256, 128], P('narrow', 'wide')
Inputs may be any that keep to these rules, and one draw needn't show every extreme that they name: `block_mask`: 0 or 1, symmetric; tokens are grouped into up to 4 chains of whole blocks in order, the first chain covering more than half of the blocks; every diagonal block is 1, and all blocks of one pair of chains share a value.
All inputs are finite; a program needn't handle non-finite values.
Results may differ from a plain program's by a relative error of at most 0.008.
Values may be sent and summed in bfloat16 or wider, within the bound.
No kernel may reach another device: no remote copies, remote signals or barrier semaphores. Data moves between devices by JAX's collectives and lax.ppermute only.
A program may use at most 64 MiB of HBM per device.

v0:
```python
import functools

import jax
import jax.numpy as jnp
from jax import lax
from jax.experimental import pallas as pl
from jax.experimental.pallas import tpu as pltpu
from jax.sharding import PartitionSpec as P

C = 128
BLOCK = 64
LANES = 128
SUB = 8
PARTS = 2


def layer_norm(values, axis):
    centre = jnp.mean(values, axis=axis, keepdims=True)
    spread = jnp.mean(jnp.square(values - centre), axis=axis, keepdims=True)
    return (values - centre) * lax.rsqrt(spread + 1e-05)


def swap_halves(values):
    flat = values.reshape(-1, LANES)
    return pltpu.roll(flat, LANES // 2, 1).reshape(values.shape)


def pack(low, high):
    lane = lax.broadcasted_iota(jnp.int32, low.shape, low.ndim - 1)
    return jnp.where(lane < LANES // 2, low, swap_halves(high))


def window_start(windowed):
    if not windowed:
        return 0
    return jnp.where(lax.axis_index("wide") * SUB < 3 * BLOCK, 0, BLOCK)


def chunks_of(rows):
    return ((0, LANES), (LANES, rows - LANES))


def project_kernel(mask_hbm, x_hbm, wl_hbm, wr_hbm, *refs):
    whole_ref, window_ref, normed_ref, cut_ref, mask_ref, x_ref, w_ref, edge, sems = refs
    group_size = whole_ref.shape[0]
    tokens = x_ref.shape[0] // SUB
    copies = [
        pltpu.make_async_copy(mask_hbm, mask_ref, sems.at[0]),
        pltpu.make_async_copy(wl_hbm, w_ref.at[0], sems.at[1]),
        pltpu.make_async_copy(wr_hbm, w_ref.at[1], sems.at[2]),
    ]
    for index in range(2):
        part = pl.ds(index * LANES * SUB, LANES * SUB)
        copies.append(pltpu.make_async_copy(x_hbm.at[part], x_ref.at[part], sems.at[3 + index]))
    for copy in copies:
        copy.start()
    copies[0].wait()
    cut = mask_ref[0, 3] == 0
    cut_ref[0] = cut.astype(jnp.int32)
    column_block = lax.axis_index("wide") * SUB // BLOCK
    kept = [mask_ref[block, column_block].astype(jnp.float32) for block in range(mask_hbm.shape[0])]
    copies[1].wait()
    copies[2].wait()
    weights = jnp.concatenate([w_ref[0].T, w_ref[1].T], axis=0)

    def project(windowed, send_ref):
        first = window_start(windowed)
        row_block = (first + lax.broadcasted_iota(jnp.int32, (1, 2 * LANES), 1)) // BLOCK
        mask = jnp.zeros((1, 2 * LANES), jnp.float32)
        for block, value in enumerate(kept):
            mask = jnp.where(row_block == block, value, mask)
        if windowed:
            copies[3].wait()
            copies[4].wait()
        chunks = chunks_of(3 * BLOCK if windowed else tokens)
        for index, (low, count) in enumerate(chunks):
            if not windowed:
                copies[3 + index].wait()
            group = 2 * LANES // count
            chunk_mask = jnp.concatenate([mask[:, low : low + count]] * group, axis=1)
            base = pl.multiple_of((first + low) * SUB, SUB)
            for start in range(0, SUB, group):
                x = [x_ref[pl.ds(base + start + k, count, stride=SUB), :] for k in range(group)]
                normed = layer_norm(jnp.concatenate(x, axis=0), 1).astype(jnp.bfloat16)
                for k in range(group):
                    normed_ref[start + k, low : low + count, :] = normed[k * count : (k + 1) * count]
                mixed = lax.dot_general(
                    weights, normed, (((1,), (1,)), ((), ())), preferred_element_type=jnp.float32
                )
                for side in range(2):
                    gate = mixed[2 * side * C : (2 * side + 1) * C]
                    value = mixed[(2 * side + 1) * C : (2 * side + 2) * C]
                    proj = jax.nn.sigmoid(gate) * value * chunk_mask
                    for k in range(group):
                        at = k * count // LANES * LANES
                        piece = proj[:, at : at + LANES]
                        if k * count % LANES:
                            piece = swap_halves(piece)
                        edge[side, index, pl.ds(start + k, C, stride=SUB), :] = piece
        part = C // group_size * SUB
        low = 0
        for side in range(2):
            for index, (_, count) in enumerate(chunks):
                values = edge[side, index].reshape(group_size, part, LANES)
                if count < LANES:
                    values = pack(values[:, : part // 2], values[:, part // 2 :])
                send_ref[:, low : low + values.shape[1], :] = values.astype(jnp.bfloat16)
                low += values.shape[1]

    pl.when(cut)(lambda: project(True, window_ref))
    pl.when(jnp.logical_not(cut))(lambda: project(False, whole_ref))


def triangle_kernel(windowed, recv_ref, send_ref):
    group_size = recv_ref.shape[0]
    wide = send_ref.shape[0]
    per_device = C // group_size
    part = per_device * SUB
    columns = group_size * SUB
    half = per_device // 2

    def load(side, channel):
        parts = []
        for index in range(2):
            start = side * send_ref.shape[1] + index * part
            swap = windowed and index == 1 and channel >= half
            at = start + (channel - half if swap else channel) * SUB
            pair = recv_ref[:, at : at + 2 * SUB, :].astype(jnp.float32)
            if swap:
                pair = swap_halves(pair)
            parts.append([
                pair[:, low : low + SUB].reshape(columns, LANES).astype(jnp.bfloat16)
                for low in (0, SUB)
            ])
        return [jnp.concatenate([p[n] for p in parts], axis=1) for n in range(2)]

    def product(right, left):
        return lax.dot_general(
            right, left, (((0,), (0,)), ((), ())), preferred_element_type=jnp.float32
        )

    cut = 3 * BLOCK
    columns_first = lax.axis_index("wide") // group_size * columns
    column = columns_first + lax.broadcasted_iota(jnp.int32, (columns, 1), 0)
    sums = []
    for channel in range(0, per_device, 2):
        for left, right in zip(load(0, channel), load(1, channel)):
            if windowed:
                above = product(right, jnp.where(column < cut, left, 0))[:cut]
                below = product(right[:, LANES:], jnp.where(column < cut, 0, left))
                sums.append(jnp.concatenate([above, below[: wide * SUB - cut]], axis=0))
            else:
                sums.append(product(right, left))
    first = [s[:, :LANES] for s in sums]
    second = [s[:, LANES:] for s in sums]
    if windowed:
        second = [pack(second[c], second[c + half]) for c in range(half)]
    start = 0
    for channels in (first, second):
        for channel in range(0, len(channels), 2):
            pair = [channels[channel + n].reshape(wide, SUB, LANES) for n in range(2)]
            pair = jnp.concatenate(pair, axis=1).astype(jnp.bfloat16)
            send_ref[:, start : start + 2 * SUB, :] = pair
            start += 2 * SUB


def update_kernel(windowed, recv_ref, normed_ref, wg_ref, wo_ref, out_hbm, tri, out_ref, sems):
    group_size = recv_ref.shape[0] // PARTS
    part = C // group_size * SUB
    rows = 3 * BLOCK if windowed else normed_ref.shape[1]
    chunks = chunks_of(rows)
    first = window_start(windowed)
    copies = []
    if windowed:
        rest = out_hbm.shape[0] - rows * SUB
        to = pl.multiple_of(jnp.where(first == 0, rows, 0) * SUB, SUB)
        out_ref[rows * SUB :, :] = jnp.zeros((rest, C), jnp.float32)
        copies.append(
            pltpu.make_async_copy(
                out_ref.at[pl.ds(rows * SUB, rest)], out_hbm.at[pl.ds(to, rest)], sems.at[2]
            )
        )
        copies[0].start()
    for index, (low, count) in enumerate(chunks):
        height = part * count // LANES
        sums = [
            recv_ref[n * group_size : (n + 1) * group_size, index * part : index * part + height, :]
            for n in range(PARTS)
        ]
        sums = sum(values.astype(jnp.float32) for values in sums)
        if count < LANES:
            sums = jnp.concatenate([sums, swap_halves(sums)], axis=1)
        tri[index] = layer_norm(sums.reshape(C, SUB, LANES), 0).reshape(C * SUB, LANES)
        for j in range(SUB):
            tri_normed = tri[index, pl.ds(j, C, stride=SUB), :].astype(jnp.bfloat16)
            mixed = lax.dot_general(
                tri_normed, wo_ref[...], (((0,), (0,)), ((), ())), preferred_element_type=jnp.float32
            )
            normed = normed_ref[j, low : low + count, :]
            gate = jax.nn.sigmoid(
                jnp.dot(normed, wg_ref[...], preferred_element_type=jnp.float32)
            )
            out_ref[pl.ds(low * SUB + j, count, stride=SUB), :] = gate * mixed[:count]
        to = pl.multiple_of((first + low) * SUB, SUB)
        copies.append(
            pltpu.make_async_copy(
                out_ref.at[pl.ds(low * SUB, count * SUB)],
                out_hbm.at[pl.ds(to, count * SUB)],
                sems.at[index],
            )
        )
        copies[-1].start()
    for copy in copies:
        copy.wait()


HBM = pl.BlockSpec(memory_space=pltpu.HBM)
VMEM = pl.BlockSpec(memory_space=pltpu.VMEM)
PARAMS = pltpu.CompilerParams(vmem_limit_bytes=48 * 1024 * 1024)


def in_hbm(array):
    return pltpu.with_memory_space_constraint(array, pltpu.HBM)


def exchange(array):
    wide, size = lax.axis_size("wide"), array.shape[0]
    groups = [list(range(first, first + size)) for first in range(0, wide, size)]
    return lax.all_to_all(
        array, "wide", split_axis=0, concat_axis=0, axis_index_groups=groups, tiled=True
    )


def after_projection(windowed, whole, window, normed, gate_weight, out_weight):
    send = window if windowed else whole
    group_size, both, _ = send.shape
    wide = group_size * PARTS
    tokens = normed.shape[1]
    back = pl.pallas_call(
        functools.partial(triangle_kernel, windowed),
        out_shape=jax.ShapeDtypeStruct((wide, both // 2, LANES), jnp.bfloat16),
        in_specs=[VMEM],
        out_specs=VMEM,
        compiler_params=PARAMS,
        name="triangle",
    )(exchange(send))
    return pl.pallas_call(
        functools.partial(update_kernel, windowed),
        out_shape=pltpu.HBM((tokens * SUB, C), jnp.float32),
        in_specs=[VMEM] * 4,
        out_specs=HBM,
        scratch_shapes=[
            pltpu.VMEM((2, C * SUB, LANES), jnp.float32),
            pltpu.VMEM((tokens * SUB, C), jnp.float32),
            pltpu.SemaphoreType.DMA((3,)),
        ],
        compiler_params=PARAMS,
        name="update",
    )(exchange(back), normed, gate_weight, out_weight)


def kernels_on_device(pair_act, block_mask, left_weight, right_weight, gate_weight, out_weight):
    tokens = pair_act.shape[0]
    wide = lax.axis_size("wide")
    group_size = wide // PARTS
    both = lambda rows: 2 * rows * (C // group_size) * SUB // LANES
    whole, window, normed, cut = pl.pallas_call(
        project_kernel,
        out_shape=(
            jax.ShapeDtypeStruct((group_size, both(tokens), LANES), jnp.bfloat16),
            jax.ShapeDtypeStruct((group_size, both(3 * BLOCK), LANES), jnp.bfloat16),
            jax.ShapeDtypeStruct((SUB, tokens, C), jnp.bfloat16),
            pltpu.SMEM((1,), jnp.int32),
        ),
        in_specs=[HBM] * 4,
        out_specs=(VMEM, VMEM, VMEM, pl.BlockSpec(memory_space=pltpu.SMEM)),
        scratch_shapes=[
            pltpu.SMEM(block_mask.shape, jnp.int32),
            pltpu.VMEM((tokens * SUB, C), jnp.float32),
            pltpu.VMEM((2, C, 2 * C), jnp.bfloat16),
            pltpu.VMEM((2, 2, C * SUB, LANES), jnp.float32),
            pltpu.SemaphoreType.DMA((5,)),
        ],
        compiler_params=PARAMS,
        name="project",
    )(
        in_hbm(block_mask),
        in_hbm(pair_act.reshape(tokens * SUB, C)),
        in_hbm(left_weight),
        in_hbm(right_weight),
    )
    update = lax.switch(
        cut[0],
        [functools.partial(after_projection, windowed) for windowed in (False, True)],
        whole,
        window,
        normed,
        gate_weight,
        out_weight,
    )
    return update.reshape(tokens, SUB, C)


def plain_on_device(pair_act, block_mask, left_weight, right_weight, gate_weight, out_weight):
    tile_rows = pair_act.shape[0]
    tile_cols = pair_act.shape[1]
    wide = lax.axis_size("wide")
    narrow = lax.axis_size("narrow")
    per_device = C // wide
    row_ids = lax.axis_index("narrow") * tile_rows + jnp.arange(tile_rows, dtype=jnp.int32)
    col_ids = lax.axis_index("wide") * tile_cols + jnp.arange(tile_cols, dtype=jnp.int32)
    block_ids = jnp.arange(block_mask.shape[0], dtype=jnp.int32)
    row_hot = (row_ids[:, None] // BLOCK == block_ids[None, :]).astype(jnp.float32)
    col_hot = (col_ids[:, None] // BLOCK == block_ids[None, :]).astype(jnp.float32)
    tile_mask = jnp.dot(jnp.dot(row_hot, block_mask.astype(jnp.float32)), col_hot.T).T
    normed = layer_norm(pair_act, -1).astype(jnp.bfloat16)

    def edges(weight):
        mixed = jnp.einsum("cd,ikc->dki", weight, normed, preferred_element_type=jnp.float32)
        proj = jax.nn.sigmoid(mixed[:C]) * mixed[C:] * tile_mask[None]
        return proj.astype(jnp.bfloat16).reshape(wide, per_device, tile_cols, tile_rows)

    send = jnp.stack([edges(left_weight), edges(right_weight)], axis=1)
    recv = lax.all_to_all(send, "wide", split_axis=0, concat_axis=0, tiled=True)
    left, right = recv[:, 0], recv[:, 1]
    if narrow > 1:
        right = lax.all_gather(right, "narrow", axis=3, tiled=True)
    tri = jnp.einsum("sckj,scki->cji", right, left, preferred_element_type=jnp.float32)
    back = tri.astype(jnp.bfloat16).reshape(per_device, wide, tile_cols, tile_rows)
    back = jnp.transpose(back, (1, 0, 2, 3))
    tri = lax.all_to_all(back, "wide", split_axis=0, concat_axis=0, tiled=True)
    tri = tri.reshape(C, tile_cols, tile_rows).astype(jnp.float32)
    tri_normed = layer_norm(tri, 0).astype(jnp.bfloat16)
    gate = jax.nn.sigmoid(
        jnp.einsum("ikc,cd->ikd", normed, gate_weight, preferred_element_type=jnp.float32)
    )
    return gate * jnp.einsum(
        "cji,cd->ijd", tri_normed, out_weight, preferred_element_type=jnp.float32
    )


def on_device(pair_act, block_mask, *weights):
    rows, cols = pair_act.shape[:2]
    blocks = block_mask.shape[0]
    fits = rows == 2 * LANES and cols == SUB and C // lax.axis_size("wide") == 4 and blocks == 4
    if lax.axis_size("narrow") > 1 or not fits:
        return plain_on_device(pair_act, block_mask, *weights)
    return kernels_on_device(pair_act, block_mask, *weights)


def solution(mesh):
    return jax.shard_map(
        on_device,
        mesh=mesh,
        in_specs=(P("narrow", "wide", None), P(), P(), P(), P(), P()),
        out_specs=P("narrow", "wide", None),
        check_vma=False,
    )
```

profile of v0, /device:TPU:0, one launch (start us, length us, event | category | flops | bytes accessed | tf_op | source)
XLA Modules:
  0.0 56.2 jit_solution(452949705618807871)
XLA Ops:
  0.0 0.0 copy-start
  0.0 0.0 copy-start.1
  0.0 2.6 %project.1 = (bf16[16,256,128]{2,1,0:T(8,128)(2,1)S(1)}, bf16[16,192,128]{2,1,0:T(8,128)(2,1)S(1)}, bf16[8,256,128]{2,1,0:T(8,128)(2,1)S(1)}, s32[1]{0:T(128)S(4)}) custom-call(s32[4,4]{1,0:T(4,128)} %mask_hbm.1, f32[2048,128]{1,0:T(8,128)} %bitcast.4, bf16[128,256]{1,0:T(8,128)(2,1)} %wl_hbm.1, bf16[128,256]{1,0:T(8,128)(2,1)} %wr_hbm.1), custom_call_target="tpu_custom_call" | custom-call | tf_op jit(solution)/shard_map/project/pallas_call | solution.py:267
  2.6 0.0 copy-done
  2.7 0.0 copy-done.1
  2.7 53.5 %conditional.1 = (f32[256,8,128]{2,1,0:T(8,128)}) conditional(s32[]{:T(128)} %bitcast.3, (bf16[16,256,128]{2,1,0:T(8,128)(2,1)S(1)}, bf16[8,256,128]{2,1,0:T(8,128)(2,1)S(1)}, bf16[128,128]{1,0:T(8,128)(2,1)S(1)}, bf16[128,128]{1,0:T(8,128)(2,1)S(1)}) %tuple.21, (bf16[16,192,128]{2,1,0:T(8,128)(2,1)S(1)}, bf16[8,256,128]{2,1,0:T(8,128)(2,1)S(1)}, ...), branch_computations={%region_0.0_spmd, %region_1.0_spmd} | conditional | bytes 4194312 | solution.py:292
  2.7 22.3 %all_to_all.16.recv_ref = bf16[16,256,128]{2,1,0:T(8,128)(2,1)S(1)} all-to-all(bf16[16,256,128]{2,1,0:T(8,128)(2,1)S(1)} %get-tuple-element.25), channel_id=1, replica_groups={{0,1,2,3,4,5,6,7,8,9,10,11,12,13,14,15},{16,17,18,19,20,21,22,23,24,25,..., dimensions={0} | all-to-all | bytes 2097152 | tf_op jit(solution)/shard_map/cond/branch_0_fun/all_to_all | solution.py:229
  24.9 0.5 triangle.2
  25.4 29.0 %all_to_all.17.recv_ref = bf16[32,128,128]{2,1,0:T(8,128)(2,1)S(1)} all-to-all(bf16[32,128,128]{2,1,0:T(8,128)(2,1)S(1)} %triangle.2), channel_id=1, replica_groups={{0,1,2,3,4,5,6,7,8,9,10,11,12,13,14,15,16,17,18,19,20,21,22,23,24,25,26..., dimensions={0} | all-to-all | bytes 2097152 | tf_op jit(solution)/shard_map/cond/branch_0_fun/all_to_all | solution.py:229
  54.4 1.8 %update.2 = f32[2048,128]{1,0:T(8,128)} custom-call(bf16[32,128,128]{2,1,0:T(8,128)(2,1)S(1)} %all_to_all.17.recv_ref, bf16[8,256,128]{2,1,0:T(8,128)(2,1)S(1)} %get-tuple-element.26.normed_ref, bf16[128,128]{1,0:T(8,128)(2,1)S(1)} %get-tuple-element.27.wg_ref, bf16[128,128]{1,0:T(8,128)(2,1)S(1)} %get-tuple-element.28.wo_ref), custom_call_target="tpu_custom_call" | custom-call | tf_op jit(solution)/shard_map/cond/branch_0_fun/update/pallas_call | solution.py:247
Async XLA Ops:
  0.0 2.6 %copy-start = (bf16[128,128]{1,0:T(8,128)(2,1)S(1)}, bf16[128,128]{1,0:T(8,128)(2,1)}, u32[]{:S(2)}) copy-start(bf16[128,128]{1,0:T(8,128)(2,1)} %param.12) | copy-start | bytes 98308
  0.0 2.7 %copy-start.1 = (bf16[128,128]{1,0:T(8,128)(2,1)S(1)}, bf16[128,128]{1,0:T(8,128)(2,1)}, u32[]{:S(2)}) copy-start(bf16[128,128]{1,0:T(8,128)(2,1)} %param.13) | copy-start | bytes 98308
where the time goes:
time: 56.4 us; the launch traced here: 56.2 us
  blocking collectives  51.3 us (91%)
  Pallas kernels  4.86 us (9%)
    all_to_all x2, blocking collectives, exchange(): lax.all_to_all(array, 'wide', split_axis=0, concat_axis=0, axis_index_gro...  51.3 us
    pallas_call x1, Pallas kernels, kernels_on_device(): pl.pallas_call(project_kernel, out_shape=(jax.ShapeDtypeStruct((group_siz...  2.63 us
    pallas_call x1, Pallas kernels, after_projection(): pl.pallas_call(functools.partial(update_kernel, windowed), out_shape=pltp...  1.77 us

commit v1 on v0

--- a/solution.py
+++ b/solution.py
@@ -38,6 +38,18 @@
 
 def chunks_of(rows):
     return ((0, LANES), (LANES, rows - LANES))
+
+
+def channel_mean(values):
+    high = values.astype(jnp.bfloat16)
+    low = (values - high.astype(jnp.float32)).astype(jnp.bfloat16)
+    ones = jnp.full((2 * C, C), 1 / C, jnp.bfloat16)
+    return jnp.dot(jnp.concatenate([high, low], axis=1), ones, preferred_element_type=jnp.float32)
+
+
+def channel_norm(values):
+    centred = values - channel_mean(values)
+    return centred * lax.rsqrt(channel_mean(jnp.square(centred)) + 1e-05)
 
 
 def project_kernel(mask_hbm, x_hbm, wl_hbm, wr_hbm, *refs):
@@ -81,7 +93,7 @@
             base = pl.multiple_of((first + low) * SUB, SUB)
             for start in range(0, SUB, group):
                 x = [x_ref[pl.ds(base + start + k, count, stride=SUB), :] for k in range(group)]
-                normed = layer_norm(jnp.concatenate(x, axis=0), 1).astype(jnp.bfloat16)
+                normed = channel_norm(jnp.concatenate(x, axis=0)).astype(jnp.bfloat16)
                 for k in range(group):
                     normed_ref[start + k, low : low + count, :] = normed[k * count : (k + 1) * count]
                 mixed = lax.dot_general(

time: 56.4 us -> 57.7 us (1.023)
  Pallas kernels: 4.86 us -> 6.18 us
    pallas_call x1, Pallas kernels: 2.63 us -> 3.95 us  [kernels_on_device(): pl.pallas_call(project_kernel, out_shape=(jax.ShapeDtypeStruct((group_siz...]
where the time goes in v1:
time: 57.7 us; the launch traced here: 57.5 us
  blocking collectives  51.2 us (89%)
  Pallas kernels  6.18 us (11%)
    all_to_all x2, blocking collectives, exchange(): lax.all_to_all(array, 'wide', split_axis=0, concat_axis=0, axis_index_gro...  51.2 us
    pallas_call x1, Pallas kernels, kernels_on_device(): pl.pallas_call(project_kernel, out_shape=(jax.ShapeDtypeStruct((group_siz...  3.95 us
    pallas_call x1, Pallas kernels, after_projection(): pl.pallas_call(functools.partial(update_kernel, windowed), out_shape=pltp...  1.77 us

profile of v1, /device:TPU:0, one launch (start us, length us, event | category | flops | bytes accessed | tf_op | source)
XLA Modules:
  0.0 57.5 jit_solution(11942374599328449542)
XLA Ops:
  0.0 0.0 copy-start
  0.0 0.0 copy-start.1
  0.0 3.9 %project.1 = (bf16[16,256,128]{2,1,0:T(8,128)(2,1)S(1)}, bf16[16,192,128]{2,1,0:T(8,128)(2,1)S(1)}, bf16[8,256,128]{2,1,0:T(8,128)(2,1)S(1)}, s32[1]{0:T(128)S(4)}) custom-call(s32[4,4]{1,0:T(4,128)} %mask_hbm.1, f32[2048,128]{1,0:T(8,128)} %bitcast.4, bf16[128,256]{1,0:T(8,128)(2,1)} %wl_hbm.1, bf16[128,256]{1,0:T(8,128)(2,1)} %wr_hbm.1), custom_call_target="tpu_custom_call" | custom-call | tf_op jit(solution)/shard_map/project/pallas_call | solution.py:279
  4.0 0.0 copy-done
  4.0 0.0 copy-done.1
  4.0 53.5 %conditional.1 = (f32[256,8,128]{2,1,0:T(8,128)}) conditional(s32[]{:T(128)} %bitcast.3, (bf16[16,256,128]{2,1,0:T(8,128)(2,1)S(1)}, bf16[8,256,128]{2,1,0:T(8,128)(2,1)S(1)}, bf16[128,128]{1,0:T(8,128)(2,1)S(1)}, bf16[128,128]{1,0:T(8,128)(2,1)S(1)}) %tuple.21, (bf16[16,192,128]{2,1,0:T(8,128)(2,1)S(1)}, bf16[8,256,128]{2,1,0:T(8,128)(2,1)S(1)}, ...), branch_computations={%region_0.0_spmd, %region_1.0_spmd} | conditional | bytes 4194312 | solution.py:304
  4.0 22.3 %all_to_all.16.recv_ref = bf16[16,256,128]{2,1,0:T(8,128)(2,1)S(1)} all-to-all(bf16[16,256,128]{2,1,0:T(8,128)(2,1)S(1)} %get-tuple-element.25), channel_id=1, replica_groups={{0,1,2,3,4,5,6,7,8,9,10,11,12,13,14,15},{16,17,18,19,20,21,22,23,24,25,..., dimensions={0} | all-to-all | bytes 2097152 | tf_op jit(solution)/shard_map/cond/branch_0_fun/all_to_all | solution.py:241
  26.3 0.5 triangle.2
  26.7 29.0 %all_to_all.17.recv_ref = bf16[32,128,128]{2,1,0:T(8,128)(2,1)S(1)} all-to-all(bf16[32,128,128]{2,1,0:T(8,128)(2,1)S(1)} %triangle.2), channel_id=1, replica_groups={{0,1,2,3,4,5,6,7,8,9,10,11,12,13,14,15,16,17,18,19,20,21,22,23,24,25,26..., dimensions={0} | all-to-all | bytes 2097152 | tf_op jit(solution)/shard_map/cond/branch_0_fun/all_to_all | solution.py:241
  55.7 1.8 %update.2 = f32[2048,128]{1,0:T(8,128)} custom-call(bf16[32,128,128]{2,1,0:T(8,128)(2,1)S(1)} %all_to_all.17.recv_ref, bf16[8,256,128]{2,1,0:T(8,128)(2,1)S(1)} %get-tuple-element.26.normed_ref, bf16[128,128]{1,0:T(8,128)(2,1)S(1)} %get-tuple-element.27.wg_ref, bf16[128,128]{1,0:T(8,128)(2,1)S(1)} %get-tuple-element.28.wo_ref), custom_call_target="tpu_custom_call" | custom-call | tf_op jit(solution)/shard_map/cond/branch_0_fun/update/pallas_call | solution.py:259
Async XLA Ops:
  0.0 4.0 %copy-start = (bf16[128,128]{1,0:T(8,128)(2,1)S(1)}, bf16[128,128]{1,0:T(8,128)(2,1)}, u32[]{:S(2)}) copy-start(bf16[128,128]{1,0:T(8,128)(2,1)} %param.12) | copy-start | bytes 98308
  0.0 4.0 %copy-start.1 = (bf16[128,128]{1,0:T(8,128)(2,1)S(1)}, bf16[128,128]{1,0:T(8,128)(2,1)}, u32[]{:S(2)}) copy-start(bf16[128,128]{1,0:T(8,128)(2,1)} %param.13) | copy-start | bytes 98308

commit v2 on v0

--- a/solution.py
+++ b/solution.py
@@ -181,6 +181,14 @@
             )
         )
         copies[0].start()
+    zeros = jnp.zeros((C, C), jnp.bfloat16)
+    weights = jnp.concatenate(
+        [
+            jnp.concatenate([wg_ref[...], zeros], axis=1),
+            jnp.concatenate([zeros, wo_ref[...]], axis=1),
+        ],
+        axis=0,
+    )
     for index, (low, count) in enumerate(chunks):
         height = part * count // LANES
         sums = [
@@ -192,15 +200,15 @@
             sums = jnp.concatenate([sums, swap_halves(sums)], axis=1)
         tri[index] = layer_norm(sums.reshape(C, SUB, LANES), 0).reshape(C * SUB, LANES)
         for j in range(SUB):
-            tri_normed = tri[index, pl.ds(j, C, stride=SUB), :].astype(jnp.bfloat16)
-            mixed = lax.dot_general(
-                tri_normed, wo_ref[...], (((0,), (0,)), ((), ())), preferred_element_type=jnp.float32
+            tri_normed = tri[index, pl.ds(j, C, stride=SUB), :].astype(jnp.bfloat16).T
+            normed = normed_ref[j, low : low + count, :]
+            mixed = jnp.dot(
+                jnp.concatenate([normed, tri_normed[:count]], axis=1),
+                weights,
+                preferred_element_type=jnp.float32,
             )
-            normed = normed_ref[j, low : low + count, :]
-            gate = jax.nn.sigmoid(
-                jnp.dot(normed, wg_ref[...], preferred_element_type=jnp.float32)
-            )
-            out_ref[pl.ds(low * SUB + j, count, stride=SUB), :] = gate * mixed[:count]
+            update = jax.nn.sigmoid(mixed[:, :C]) * mixed[:, C:]
+            out_ref[pl.ds(low * SUB + j, count, stride=SUB), :] = update
         to = pl.multiple_of((first + low) * SUB, SUB)
         copies.append(
             pltpu.make_async_copy(

time: 56.4 us -> 56.4 us (level)
  no operation moved by 1% of the time
where the time goes in v2:
time: 56.4 us; the launch traced here: 56.2 us
  blocking collectives  51.3 us (91%)
  Pallas kernels  4.88 us (9%)
    all_to_all x2, blocking collectives, exchange(): lax.all_to_all(array, 'wide', split_axis=0, concat_axis=0, axis_index_gro...  51.3 us
    pallas_call x1, Pallas kernels, kernels_on_device(): pl.pallas_call(project_kernel, out_shape=(jax.ShapeDtypeStruct((group_siz...  2.63 us
    pallas_call x1, Pallas kernels, after_projection(): pl.pallas_call(functools.partial(update_kernel, windowed), out_shape=pltp...  1.78 us

profile of v2, /device:TPU:0, one launch (start us, length us, event | category | flops | bytes accessed | tf_op | source)
XLA Modules:
  0.0 56.2 jit_solution(11376113001184487959)
XLA Ops:
  0.0 0.0 copy-start
  0.0 0.0 copy-start.1
  0.0 2.6 %project.1 = (bf16[16,256,128]{2,1,0:T(8,128)(2,1)S(1)}, bf16[16,192,128]{2,1,0:T(8,128)(2,1)S(1)}, bf16[8,256,128]{2,1,0:T(8,128)(2,1)S(1)}, s32[1]{0:T(128)S(4)}) custom-call(s32[4,4]{1,0:T(4,128)} %mask_hbm.1, f32[2048,128]{1,0:T(8,128)} %bitcast.4, bf16[128,256]{1,0:T(8,128)(2,1)} %wl_hbm.1, bf16[128,256]{1,0:T(8,128)(2,1)} %wr_hbm.1), custom_call_target="tpu_custom_call" | custom-call | tf_op jit(solution)/shard_map/project/pallas_call | solution.py:275
  2.6 0.0 copy-done
  2.7 0.0 copy-done.1
  2.7 53.5 %conditional.1 = (f32[256,8,128]{2,1,0:T(8,128)}) conditional(s32[]{:T(128)} %bitcast.3, (bf16[16,256,128]{2,1,0:T(8,128)(2,1)S(1)}, bf16[8,256,128]{2,1,0:T(8,128)(2,1)S(1)}, bf16[128,128]{1,0:T(8,128)(2,1)S(1)}, bf16[128,128]{1,0:T(8,128)(2,1)S(1)}) %tuple.21, (bf16[16,192,128]{2,1,0:T(8,128)(2,1)S(1)}, bf16[8,256,128]{2,1,0:T(8,128)(2,1)S(1)}, ...), branch_computations={%region_0.0_spmd, %region_1.0_spmd} | conditional | bytes 4194312 | solution.py:300
  2.7 22.3 %all_to_all.16.recv_ref = bf16[16,256,128]{2,1,0:T(8,128)(2,1)S(1)} all-to-all(bf16[16,256,128]{2,1,0:T(8,128)(2,1)S(1)} %get-tuple-element.25), channel_id=1, replica_groups={{0,1,2,3,4,5,6,7,8,9,10,11,12,13,14,15},{16,17,18,19,20,21,22,23,24,25,..., dimensions={0} | all-to-all | bytes 2097152 | tf_op jit(solution)/shard_map/cond/branch_0_fun/all_to_all | solution.py:237
  24.9 0.5 triangle.2
  25.4 29.0 %all_to_all.17.recv_ref = bf16[32,128,128]{2,1,0:T(8,128)(2,1)S(1)} all-to-all(bf16[32,128,128]{2,1,0:T(8,128)(2,1)S(1)} %triangle.2), channel_id=1, replica_groups={{0,1,2,3,4,5,6,7,8,9,10,11,12,13,14,15,16,17,18,19,20,21,22,23,24,25,26..., dimensions={0} | all-to-all | bytes 2097152 | tf_op jit(solution)/shard_map/cond/branch_0_fun/all_to_all | solution.py:237
  54.4 1.8 %update.2 = f32[2048,128]{1,0:T(8,128)} custom-call(bf16[32,128,128]{2,1,0:T(8,128)(2,1)S(1)} %all_to_all.17.recv_ref, bf16[8,256,128]{2,1,0:T(8,128)(2,1)S(1)} %get-tuple-element.26.normed_ref, bf16[128,128]{1,0:T(8,128)(2,1)S(1)} %get-tuple-element.27.wg_ref, bf16[128,128]{1,0:T(8,128)(2,1)S(1)} %get-tuple-element.28.wo_ref), custom_call_target="tpu_custom_call" | custom-call | tf_op jit(solution)/shard_map/cond/branch_0_fun/update/pallas_call | solution.py:255
Async XLA Ops:
  0.0 2.6 %copy-start = (bf16[128,128]{1,0:T(8,128)(2,1)S(1)}, bf16[128,128]{1,0:T(8,128)(2,1)}, u32[]{:S(2)}) copy-start(bf16[128,128]{1,0:T(8,128)(2,1)} %param.12) | copy-start | bytes 98308
  0.0 2.7 %copy-start.1 = (bf16[128,128]{1,0:T(8,128)(2,1)S(1)}, bf16[128,128]{1,0:T(8,128)(2,1)}, u32[]{:S(2)}) copy-start(bf16[128,128]{1,0:T(8,128)(2,1)} %param.13) | copy-start | bytes 98308

commit v3 on v0

--- a/solution.py
+++ b/solution.py
@@ -43,16 +43,17 @@
 def project_kernel(mask_hbm, x_hbm, wl_hbm, wr_hbm, *refs):
     whole_ref, window_ref, normed_ref, cut_ref, mask_ref, x_ref, w_ref, edge, sems = refs
     group_size = whole_ref.shape[0]
-    tokens = x_ref.shape[0] // SUB
+    tokens = x_hbm.shape[0] // SUB
+    pieces = []
+    for index in range(tokens // BLOCK):
+        piece = pl.ds(index * BLOCK * SUB, BLOCK * SUB)
+        pieces.append(pltpu.make_async_copy(x_hbm.at[piece], x_ref.at[piece], sems.at[3 + index]))
     copies = [
         pltpu.make_async_copy(mask_hbm, mask_ref, sems.at[0]),
         pltpu.make_async_copy(wl_hbm, w_ref.at[0], sems.at[1]),
         pltpu.make_async_copy(wr_hbm, w_ref.at[1], sems.at[2]),
     ]
-    for index in range(2):
-        part = pl.ds(index * LANES * SUB, LANES * SUB)
-        copies.append(pltpu.make_async_copy(x_hbm.at[part], x_ref.at[part], sems.at[3 + index]))
-    for copy in copies:
+    for copy in copies + pieces:
         copy.start()
     copies[0].wait()
     cut = mask_ref[0, 3] == 0
@@ -69,13 +70,11 @@
         mask = jnp.zeros((1, 2 * LANES), jnp.float32)
         for block, value in enumerate(kept):
             mask = jnp.where(row_block == block, value, mask)
-        if windowed:
-            copies[3].wait()
-            copies[4].wait()
         chunks = chunks_of(3 * BLOCK if windowed else tokens)
+        needs = (3, 4) if windowed else (2, 4)
         for index, (low, count) in enumerate(chunks):
-            if not windowed:
-                copies[3 + index].wait()
+            for piece in pieces[needs[index - 1] if index else 0 : needs[index]]:
+                piece.wait()
             group = 2 * LANES // count
             chunk_mask = jnp.concatenate([mask[:, low : low + count]] * group, axis=1)
             base = pl.multiple_of((first + low) * SUB, SUB)
@@ -101,7 +100,7 @@
         low = 0
         for side in range(2):
             for index, (_, count) in enumerate(chunks):
-                values = edge[side, index].reshape(group_size, part, LANES)
+                values = edge[side, index, : C * SUB, :].reshape(group_size, part, LANES)
                 if count < LANES:
                     values = pack(values[:, : part // 2], values[:, part // 2 :])
                 send_ref[:, low : low + values.shape[1], :] = values.astype(jnp.bfloat16)
@@ -174,10 +173,10 @@
     if windowed:
         rest = out_hbm.shape[0] - rows * SUB
         to = pl.multiple_of(jnp.where(first == 0, rows, 0) * SUB, SUB)
-        out_ref[rows * SUB :, :] = jnp.zeros((rest, C), jnp.float32)
+        out_ref[pl.ds(rows * SUB, rest), :] = jnp.zeros((rest, C), jnp.float32)
         copies.append(
             pltpu.make_async_copy(
-                out_ref.at[pl.ds(rows * SUB, rest)], out_hbm.at[pl.ds(to, rest)], sems.at[2]
+                out_ref.at[pl.ds(rows * SUB, rest)], out_hbm.at[pl.ds(to, rest)], sems.at[3]
             )
         )
         copies[0].start()
@@ -190,7 +189,7 @@
         sums = sum(values.astype(jnp.float32) for values in sums)
         if count < LANES:
             sums = jnp.concatenate([sums, swap_halves(sums)], axis=1)
-        tri[index] = layer_norm(sums.reshape(C, SUB, LANES), 0).reshape(C * SUB, LANES)
+        tri[index, : C * SUB, :] = layer_norm(sums.reshape(C, SUB, LANES), 0).reshape(C * SUB, LANES)
         for j in range(SUB):
             tri_normed = tri[index, pl.ds(j, C, stride=SUB), :].astype(jnp.bfloat16)
             mixed = lax.dot_general(
@@ -201,15 +200,16 @@
                 jnp.dot(normed, wg_ref[...], preferred_element_type=jnp.float32)
             )
             out_ref[pl.ds(low * SUB + j, count, stride=SUB), :] = gate * mixed[:count]
-        to = pl.multiple_of((first + low) * SUB, SUB)
-        copies.append(
-            pltpu.make_async_copy(
-                out_ref.at[pl.ds(low * SUB, count * SUB)],
-                out_hbm.at[pl.ds(to, count * SUB)],
-                sems.at[index],
+        for piece in range(low, low + count, BLOCK):
+            to = pl.multiple_of((first + piece) * SUB, SUB)
+            copies.append(
+                pltpu.make_async_copy(
+                    out_ref.at[pl.ds(piece * SUB, BLOCK * SUB)],
+                    out_hbm.at[pl.ds(to, BLOCK * SUB)],
+                    sems.at[piece // BLOCK],
+                )
             )
-        )
-        copies[-1].start()
+            copies[-1].start()
     for copy in copies:
         copy.wait()
 
@@ -250,9 +250,9 @@
         in_specs=[VMEM] * 4,
         out_specs=HBM,
         scratch_shapes=[
-            pltpu.VMEM((2, C * SUB, LANES), jnp.float32),
-            pltpu.VMEM((tokens * SUB, C), jnp.float32),
-            pltpu.SemaphoreType.DMA((3,)),
+            pltpu.VMEM((2, C * SUB + SUB, LANES), jnp.float32),
+            pltpu.VMEM((tokens * SUB + SUB, C), jnp.float32),
+            pltpu.SemaphoreType.DMA((4,)),
         ],
         compiler_params=PARAMS,
         name="update",
@@ -276,10 +276,10 @@
         out_specs=(VMEM, VMEM, VMEM, pl.BlockSpec(memory_space=pltpu.SMEM)),
         scratch_shapes=[
             pltpu.SMEM(block_mask.shape, jnp.int32),
-            pltpu.VMEM((tokens * SUB, C), jnp.float32),
+            pltpu.VMEM((tokens * SUB + SUB, C), jnp.float32),
             pltpu.VMEM((2, C, 2 * C), jnp.bfloat16),
-            pltpu.VMEM((2, 2, C * SUB, LANES), jnp.float32),
-            pltpu.SemaphoreType.DMA((5,)),
+            pltpu.VMEM((2, 2, C * SUB + SUB, LANES), jnp.float32),
+            pltpu.SemaphoreType.DMA((7,)),
         ],
         compiler_params=PARAMS,
         name="project",

time: 56.4 us -> 48.2 us (0.85)
  blocking collectives: 51.3 us -> 42.8 us
    all_to_all x2, blocking collectives: 51.3 us -> 42.8 us  [exchange(): lax.all_to_all(array, 'wide', split_axis=0, concat_axis=0, axis_index_gro...]
where the time goes in v3:
time: 48.2 us; the launch traced here: 48 us
  blocking collectives  42.8 us (89%)
  Pallas kernels  5.11 us (11%)
    all_to_all x2, blocking collectives, exchange(): lax.all_to_all(array, 'wide', split_axis=0, concat_axis=0, axis_index_gro...  42.8 us
    pallas_call x1, Pallas kernels, kernels_on_device(): pl.pallas_call(project_kernel, out_shape=(jax.ShapeDtypeStruct((group_siz...  2.74 us
    pallas_call x1, Pallas kernels, after_projection(): pl.pallas_call(functools.partial(update_kernel, windowed), out_shape=pltp...  1.72 us

profile of v3, /device:TPU:0, one launch (start us, length us, event | category | flops | bytes accessed | tf_op | source)
XLA Modules:
  0.0 48.0 jit_solution(8480742424063992430)
XLA Ops:
  0.0 0.0 copy-start
  0.0 0.0 copy-start.1
  0.0 2.7 %project.1 = (bf16[16,256,128]{2,1,0:T(8,128)(2,1)S(1)}, bf16[16,192,128]{2,1,0:T(8,128)(2,1)S(1)}, bf16[8,256,128]{2,1,0:T(8,128)(2,1)S(1)}, s32[1]{0:T(128)S(4)}) custom-call(s32[4,4]{1,0:T(4,128)} %mask_hbm.1, f32[2048,128]{1,0:T(8,128)} %bitcast.4, bf16[128,256]{1,0:T(8,128)(2,1)} %wl_hbm.1, bf16[128,256]{1,0:T(8,128)(2,1)} %wr_hbm.1), custom_call_target="tpu_custom_call" | custom-call | tf_op jit(solution)/shard_map/project/pallas_call | solution.py:267
  2.8 0.0 copy-done
  2.8 0.0 copy-done.1
  2.8 45.2 %conditional.1 = (f32[256,8,128]{2,1,0:T(8,128)}) conditional(s32[]{:T(128)} %bitcast.3, (bf16[16,256,128]{2,1,0:T(8,128)(2,1)S(1)}, bf16[8,256,128]{2,1,0:T(8,128)(2,1)S(1)}, bf16[128,128]{1,0:T(8,128)(2,1)S(1)}, bf16[128,128]{1,0:T(8,128)(2,1)S(1)}) %tuple.21, (bf16[16,192,128]{2,1,0:T(8,128)(2,1)S(1)}, bf16[8,256,128]{2,1,0:T(8,128)(2,1)S(1)}, ...), branch_computations={%region_0.0_spmd, %region_1.0_spmd} | conditional | bytes 4194312 | solution.py:292
  2.8 19.4 %all_to_all.18.recv_ref = bf16[16,192,128]{2,1,0:T(8,128)(2,1)S(1)} all-to-all(bf16[16,192,128]{2,1,0:T(8,128)(2,1)S(1)} %get-tuple-element.29), channel_id=1, replica_groups={{0,1,2,3,4,5,6,7,8,9,10,11,12,13,14,15},{16,17,18,19,20,21,22,23,24,25,..., dimensions={0} | all-to-all | bytes 1572864 | tf_op jit(solution)/shard_map/cond/branch_1_fun/all_to_all | solution.py:229
  22.2 0.7 %triangle.3 = bf16[32,96,128]{2,1,0:T(8,128)(2,1)S(1)} custom-call(bf16[16,192,128]{2,1,0:T(8,128)(2,1)S(1)} %all_to_all.18.recv_ref), custom_call_target="tpu_custom_call" | custom-call | tf_op jit(solution)/shard_map/cond/branch_1_fun/triangle/pallas_call | solution.py:239
  22.9 23.4 %all_to_all.19.recv_ref = bf16[32,96,128]{2,1,0:T(8,128)(2,1)S(1)} all-to-all(bf16[32,96,128]{2,1,0:T(8,128)(2,1)S(1)} %triangle.3), channel_id=1, replica_groups={{0,1,2,3,4,5,6,7,8,9,10,11,12,13,14,15,16,17,18,19,20,21,22,23,24,25,26..., dimensions={0} | all-to-all | bytes 1572864 | tf_op jit(solution)/shard_map/cond/branch_1_fun/all_to_all | solution.py:229
  46.3 1.7 %update.3 = f32[2048,128]{1,0:T(8,128)} custom-call(bf16[32,96,128]{2,1,0:T(8,128)(2,1)S(1)} %all_to_all.19.recv_ref, bf16[8,256,128]{2,1,0:T(8,128)(2,1)S(1)} %get-tuple-element.30.normed_ref, bf16[128,128]{1,0:T(8,128)(2,1)S(1)} %get-tuple-element.31.wg_ref, bf16[128,128]{1,0:T(8,128)(2,1)S(1)} %get-tuple-element.32.wo_ref), custom_call_target="tpu_custom_call" | custom-call | tf_op jit(solution)/shard_map/cond/branch_1_fun/update/pallas_call | solution.py:247
Async XLA Ops:
  0.0 2.8 %copy-start = (bf16[128,128]{1,0:T(8,128)(2,1)S(1)}, bf16[128,128]{1,0:T(8,128)(2,1)}, u32[]{:S(2)}) copy-start(bf16[128,128]{1,0:T(8,128)(2,1)} %param.12) | copy-start | bytes 98308
  0.0 2.8 %copy-start.1 = (bf16[128,128]{1,0:T(8,128)(2,1)S(1)}, bf16[128,128]{1,0:T(8,128)(2,1)}, u32[]{:S(2)}) copy-start(bf16[128,128]{1,0:T(8,128)(2,1)} %param.13) | copy-start | bytes 98308

commit v4 on v0

--- a/solution.py
+++ b/solution.py
@@ -43,24 +43,21 @@
 def project_kernel(mask_hbm, x_hbm, wl_hbm, wr_hbm, *refs):
     whole_ref, window_ref, normed_ref, cut_ref, mask_ref, x_ref, w_ref, edge, sems = refs
     group_size = whole_ref.shape[0]
-    tokens = x_ref.shape[0] // SUB
+    tokens = x_hbm.shape[0] // SUB
     copies = [
-        pltpu.make_async_copy(mask_hbm, mask_ref, sems.at[0]),
-        pltpu.make_async_copy(wl_hbm, w_ref.at[0], sems.at[1]),
-        pltpu.make_async_copy(wr_hbm, w_ref.at[1], sems.at[2]),
+        pltpu.make_async_copy(x_hbm, x_ref.at[pl.ds(0, tokens * SUB)], sems.at[0]),
+        pltpu.make_async_copy(mask_hbm, mask_ref, sems.at[1]),
+        pltpu.make_async_copy(wl_hbm, w_ref.at[0], sems.at[2]),
+        pltpu.make_async_copy(wr_hbm, w_ref.at[1], sems.at[3]),
     ]
-    for index in range(2):
-        part = pl.ds(index * LANES * SUB, LANES * SUB)
-        copies.append(pltpu.make_async_copy(x_hbm.at[part], x_ref.at[part], sems.at[3 + index]))
     for copy in copies:
         copy.start()
-    copies[0].wait()
+    for copy in copies:
+        copy.wait()
     cut = mask_ref[0, 3] == 0
     cut_ref[0] = cut.astype(jnp.int32)
     column_block = lax.axis_index("wide") * SUB // BLOCK
     kept = [mask_ref[block, column_block].astype(jnp.float32) for block in range(mask_hbm.shape[0])]
-    copies[1].wait()
-    copies[2].wait()
     weights = jnp.concatenate([w_ref[0].T, w_ref[1].T], axis=0)
 
     def project(windowed, send_ref):
@@ -69,13 +66,8 @@
         mask = jnp.zeros((1, 2 * LANES), jnp.float32)
         for block, value in enumerate(kept):
             mask = jnp.where(row_block == block, value, mask)
-        if windowed:
-            copies[3].wait()
-            copies[4].wait()
         chunks = chunks_of(3 * BLOCK if windowed else tokens)
         for index, (low, count) in enumerate(chunks):
-            if not windowed:
-                copies[3 + index].wait()
             group = 2 * LANES // count
             chunk_mask = jnp.concatenate([mask[:, low : low + count]] * group, axis=1)
             base = pl.multiple_of((first + low) * SUB, SUB)
@@ -101,7 +93,7 @@
         low = 0
         for side in range(2):
             for index, (_, count) in enumerate(chunks):
-                values = edge[side, index].reshape(group_size, part, LANES)
+                values = edge[side, index, : C * SUB, :].reshape(group_size, part, LANES)
                 if count < LANES:
                     values = pack(values[:, : part // 2], values[:, part // 2 :])
                 send_ref[:, low : low + values.shape[1], :] = values.astype(jnp.bfloat16)
@@ -174,7 +166,7 @@
     if windowed:
         rest = out_hbm.shape[0] - rows * SUB
         to = pl.multiple_of(jnp.where(first == 0, rows, 0) * SUB, SUB)
-        out_ref[rows * SUB :, :] = jnp.zeros((rest, C), jnp.float32)
+        out_ref[pl.ds(rows * SUB, rest), :] = jnp.zeros((rest, C), jnp.float32)
         copies.append(
             pltpu.make_async_copy(
                 out_ref.at[pl.ds(rows * SUB, rest)], out_hbm.at[pl.ds(to, rest)], sems.at[2]
@@ -190,7 +182,7 @@
         sums = sum(values.astype(jnp.float32) for values in sums)
         if count < LANES:
             sums = jnp.concatenate([sums, swap_halves(sums)], axis=1)
-        tri[index] = layer_norm(sums.reshape(C, SUB, LANES), 0).reshape(C * SUB, LANES)
+        tri[index, : C * SUB, :] = layer_norm(sums.reshape(C, SUB, LANES), 0).reshape(C * SUB, LANES)
         for j in range(SUB):
             tri_normed = tri[index, pl.ds(j, C, stride=SUB), :].astype(jnp.bfloat16)
             mixed = lax.dot_general(
@@ -250,8 +242,8 @@
         in_specs=[VMEM] * 4,
         out_specs=HBM,
         scratch_shapes=[
-            pltpu.VMEM((2, C * SUB, LANES), jnp.float32),
-            pltpu.VMEM((tokens * SUB, C), jnp.float32),
+            pltpu.VMEM((2, C * SUB + SUB, LANES), jnp.float32),
+            pltpu.VMEM((tokens * SUB + SUB, C), jnp.float32),
             pltpu.SemaphoreType.DMA((3,)),
         ],
         compiler_params=PARAMS,
@@ -276,10 +268,10 @@
         out_specs=(VMEM, VMEM, VMEM, pl.BlockSpec(memory_space=pltpu.SMEM)),
         scratch_shapes=[
             pltpu.SMEM(block_mask.shape, jnp.int32),
-            pltpu.VMEM((tokens * SUB, C), jnp.float32),
+            pltpu.VMEM((tokens * SUB + SUB, C), jnp.float32),
             pltpu.VMEM((2, C, 2 * C), jnp.bfloat16),
-            pltpu.VMEM((2, 2, C * SUB, LANES), jnp.float32),
-            pltpu.SemaphoreType.DMA((5,)),
+            pltpu.VMEM((2, 2, C * SUB + SUB, LANES), jnp.float32),
+            pltpu.SemaphoreType.DMA((4,)),
         ],
         compiler_params=PARAMS,
         name="project",

time: 56.4 us -> 56.4 us (level)
  no operation moved by 1% of the time
where the time goes in v4:
time: 56.4 us; the launch traced here: 56.2 us
  blocking collectives  51.3 us (91%)
  Pallas kernels  4.85 us (9%)
    all_to_all x2, blocking collectives, exchange(): lax.all_to_all(array, 'wide', split_axis=0, concat_axis=0, axis_index_gro...  51.3 us
    pallas_call x1, Pallas kernels, kernels_on_device(): pl.pallas_call(project_kernel, out_shape=(jax.ShapeDtypeStruct((group_siz...  2.62 us
    pallas_call x1, Pallas kernels, after_projection(): pl.pallas_call(functools.partial(update_kernel, windowed), out_shape=pltp...  1.77 us

profile of v4, /device:TPU:0, one launch (start us, length us, event | category | flops | bytes accessed | tf_op | source)
XLA Modules:
  0.0 56.2 jit_solution(17976001612848408958)
XLA Ops:
  0.0 0.0 copy-start
  0.0 0.0 copy-start.1
  0.0 2.6 %project.1 = (bf16[16,256,128]{2,1,0:T(8,128)(2,1)S(1)}, bf16[16,192,128]{2,1,0:T(8,128)(2,1)S(1)}, bf16[8,256,128]{2,1,0:T(8,128)(2,1)S(1)}, s32[1]{0:T(128)S(4)}) custom-call(s32[4,4]{1,0:T(4,128)} %mask_hbm.1, f32[2048,128]{1,0:T(8,128)} %bitcast.4, bf16[128,256]{1,0:T(8,128)(2,1)} %wl_hbm.1, bf16[128,256]{1,0:T(8,128)(2,1)} %wr_hbm.1), custom_call_target="tpu_custom_call" | custom-call | tf_op jit(solution)/shard_map/project/pallas_call | solution.py:259
  2.6 0.0 copy-done
  2.6 0.0 copy-done.1
  2.7 53.5 %conditional.1 = (f32[256,8,128]{2,1,0:T(8,128)}) conditional(s32[]{:T(128)} %bitcast.3, (bf16[16,256,128]{2,1,0:T(8,128)(2,1)S(1)}, bf16[8,256,128]{2,1,0:T(8,128)(2,1)S(1)}, bf16[128,128]{1,0:T(8,128)(2,1)S(1)}, bf16[128,128]{1,0:T(8,128)(2,1)S(1)}) %tuple.21, (bf16[16,192,128]{2,1,0:T(8,128)(2,1)S(1)}, bf16[8,256,128]{2,1,0:T(8,128)(2,1)S(1)}, ...), branch_computations={%region_0.0_spmd, %region_1.0_spmd} | conditional | bytes 4194312 | solution.py:284
  2.7 22.3 %all_to_all.16.recv_ref = bf16[16,256,128]{2,1,0:T(8,128)(2,1)S(1)} all-to-all(bf16[16,256,128]{2,1,0:T(8,128)(2,1)S(1)} %get-tuple-element.25), channel_id=1, replica_groups={{0,1,2,3,4,5,6,7,8,9,10,11,12,13,14,15},{16,17,18,19,20,21,22,23,24,25,..., dimensions={0} | all-to-all | bytes 2097152 | tf_op jit(solution)/shard_map/cond/branch_0_fun/all_to_all | solution.py:221
  24.9 0.5 triangle.2
  25.4 29.0 %all_to_all.17.recv_ref = bf16[32,128,128]{2,1,0:T(8,128)(2,1)S(1)} all-to-all(bf16[32,128,128]{2,1,0:T(8,128)(2,1)S(1)} %triangle.2), channel_id=1, replica_groups={{0,1,2,3,4,5,6,7,8,9,10,11,12,13,14,15,16,17,18,19,20,21,22,23,24,25,26..., dimensions={0} | all-to-all | bytes 2097152 | tf_op jit(solution)/shard_map/cond/branch_0_fun/all_to_all | solution.py:221
  54.4 1.8 %update.2 = f32[2048,128]{1,0:T(8,128)} custom-call(bf16[32,128,128]{2,1,0:T(8,128)(2,1)S(1)} %all_to_all.17.recv_ref, bf16[8,256,128]{2,1,0:T(8,128)(2,1)S(1)} %get-tuple-element.26.normed_ref, bf16[128,128]{1,0:T(8,128)(2,1)S(1)} %get-tuple-element.27.wg_ref, bf16[128,128]{1,0:T(8,128)(2,1)S(1)} %get-tuple-element.28.wo_ref), custom_call_target="tpu_custom_call" | custom-call | tf_op jit(solution)/shard_map/cond/branch_0_fun/update/pallas_call | solution.py:239
Async XLA Ops:
  0.0 2.6 %copy-start = (bf16[128,128]{1,0:T(8,128)(2,1)S(1)}, bf16[128,128]{1,0:T(8,128)(2,1)}, u32[]{:S(2)}) copy-start(bf16[128,128]{1,0:T(8,128)(2,1)} %param.12) | copy-start | bytes 98308
  0.0 2.6 %copy-start.1 = (bf16[128,128]{1,0:T(8,128)(2,1)S(1)}, bf16[128,128]{1,0:T(8,128)(2,1)}, u32[]{:S(2)}) copy-start(bf16[128,128]{1,0:T(8,128)(2,1)} %param.13) | copy-start | bytes 98308

commit v5 on v0

--- a/solution.py
+++ b/solution.py
@@ -43,7 +43,7 @@
 def project_kernel(mask_hbm, x_hbm, wl_hbm, wr_hbm, *refs):
     whole_ref, window_ref, normed_ref, cut_ref, mask_ref, x_ref, w_ref, edge, sems = refs
     group_size = whole_ref.shape[0]
-    tokens = x_ref.shape[0] // SUB
+    tokens = x_hbm.shape[0] // SUB
     copies = [
         pltpu.make_async_copy(mask_hbm, mask_ref, sems.at[0]),
         pltpu.make_async_copy(wl_hbm, w_ref.at[0], sems.at[1]),
@@ -101,7 +101,7 @@
         low = 0
         for side in range(2):
             for index, (_, count) in enumerate(chunks):
-                values = edge[side, index].reshape(group_size, part, LANES)
+                values = edge[side, index, : C * SUB, :].reshape(group_size, part, LANES)
                 if count < LANES:
                     values = pack(values[:, : part // 2], values[:, part // 2 :])
                 send_ref[:, low : low + values.shape[1], :] = values.astype(jnp.bfloat16)
@@ -174,7 +174,7 @@
     if windowed:
         rest = out_hbm.shape[0] - rows * SUB
         to = pl.multiple_of(jnp.where(first == 0, rows, 0) * SUB, SUB)
-        out_ref[rows * SUB :, :] = jnp.zeros((rest, C), jnp.float32)
+        out_ref[pl.ds(rows * SUB, rest), :] = jnp.zeros((rest, C), jnp.float32)
         copies.append(
             pltpu.make_async_copy(
                 out_ref.at[pl.ds(rows * SUB, rest)], out_hbm.at[pl.ds(to, rest)], sems.at[2]
@@ -190,7 +190,7 @@
         sums = sum(values.astype(jnp.float32) for values in sums)
         if count < LANES:
             sums = jnp.concatenate([sums, swap_halves(sums)], axis=1)
-        tri[index] = layer_norm(sums.reshape(C, SUB, LANES), 0).reshape(C * SUB, LANES)
+        tri[index, : C * SUB, :] = layer_norm(sums.reshape(C, SUB, LANES), 0).reshape(C * SUB, LANES)
         for j in range(SUB):
             tri_normed = tri[index, pl.ds(j, C, stride=SUB), :].astype(jnp.bfloat16)
             mixed = lax.dot_general(
@@ -250,8 +250,8 @@
         in_specs=[VMEM] * 4,
         out_specs=HBM,
         scratch_shapes=[
-            pltpu.VMEM((2, C * SUB, LANES), jnp.float32),
-            pltpu.VMEM((tokens * SUB, C), jnp.float32),
+            pltpu.VMEM((2, C * SUB + SUB, LANES), jnp.float32),
+            pltpu.VMEM((tokens * SUB + SUB, C), jnp.float32),
             pltpu.SemaphoreType.DMA((3,)),
         ],
         compiler_params=PARAMS,
@@ -276,9 +276,9 @@
         out_specs=(VMEM, VMEM, VMEM, pl.BlockSpec(memory_space=pltpu.SMEM)),
         scratch_shapes=[
             pltpu.SMEM(block_mask.shape, jnp.int32),
-            pltpu.VMEM((tokens * SUB, C), jnp.float32),
+            pltpu.VMEM((tokens * SUB + SUB, C), jnp.float32),
             pltpu.VMEM((2, C, 2 * C), jnp.bfloat16),
-            pltpu.VMEM((2, 2, C * SUB, LANES), jnp.float32),
+            pltpu.VMEM((2, 2, C * SUB + SUB, LANES), jnp.float32),
             pltpu.SemaphoreType.DMA((5,)),
         ],
         compiler_params=PARAMS,

time: 56.4 us -> 48 us (0.85)
  blocking collectives: 51.3 us -> 42.8 us
    all_to_all x2, blocking collectives: 51.3 us -> 42.8 us  [exchange(): lax.all_to_all(array, 'wide', split_axis=0, concat_axis=0, axis_index_gro...]
where the time goes in v5:
time: 48 us; the launch traced here: 47.8 us
  blocking collectives  42.8 us (89%)
  Pallas kernels  4.9 us (10%)
    all_to_all x2, blocking collectives, exchange(): lax.all_to_all(array, 'wide', split_axis=0, concat_axis=0, axis_index_gro...  42.8 us
    pallas_call x1, Pallas kernels, kernels_on_device(): pl.pallas_call(project_kernel, out_shape=(jax.ShapeDtypeStruct((group_siz...  2.53 us
    pallas_call x1, Pallas kernels, after_projection(): pl.pallas_call(functools.partial(update_kernel, windowed), out_shape=pltp...  1.71 us

profile of v5, /device:TPU:0, one launch (start us, length us, event | category | flops | bytes accessed | tf_op | source)
XLA Modules:
  0.0 47.8 jit_solution(7551665938440908437)
XLA Ops:
  0.0 0.0 copy-start
  0.0 0.0 copy-start.1
  0.0 2.5 %project.1 = (bf16[16,256,128]{2,1,0:T(8,128)(2,1)S(1)}, bf16[16,192,128]{2,1,0:T(8,128)(2,1)S(1)}, bf16[8,256,128]{2,1,0:T(8,128)(2,1)S(1)}, s32[1]{0:T(128)S(4)}) custom-call(s32[4,4]{1,0:T(4,128)} %mask_hbm.1, f32[2048,128]{1,0:T(8,128)} %bitcast.4, bf16[128,256]{1,0:T(8,128)(2,1)} %wl_hbm.1, bf16[128,256]{1,0:T(8,128)(2,1)} %wr_hbm.1), custom_call_target="tpu_custom_call" | custom-call | tf_op jit(solution)/shard_map/project/pallas_call | solution.py:267
  2.6 0.0 copy-done
  2.6 0.0 copy-done.1
  2.6 45.2 %conditional.1 = (f32[256,8,128]{2,1,0:T(8,128)}) conditional(s32[]{:T(128)} %bitcast.3, (bf16[16,256,128]{2,1,0:T(8,128)(2,1)S(1)}, bf16[8,256,128]{2,1,0:T(8,128)(2,1)S(1)}, bf16[128,128]{1,0:T(8,128)(2,1)S(1)}, bf16[128,128]{1,0:T(8,128)(2,1)S(1)}) %tuple.21, (bf16[16,192,128]{2,1,0:T(8,128)(2,1)S(1)}, bf16[8,256,128]{2,1,0:T(8,128)(2,1)S(1)}, ...), branch_computations={%region_0.0_spmd, %region_1.0_spmd} | conditional | bytes 4194312 | solution.py:292
  2.6 19.4 %all_to_all.18.recv_ref = bf16[16,192,128]{2,1,0:T(8,128)(2,1)S(1)} all-to-all(bf16[16,192,128]{2,1,0:T(8,128)(2,1)S(1)} %get-tuple-element.29), channel_id=1, replica_groups={{0,1,2,3,4,5,6,7,8,9,10,11,12,13,14,15},{16,17,18,19,20,21,22,23,24,25,..., dimensions={0} | all-to-all | bytes 1572864 | tf_op jit(solution)/shard_map/cond/branch_1_fun/all_to_all | solution.py:229
  22.0 0.7 %triangle.3 = bf16[32,96,128]{2,1,0:T(8,128)(2,1)S(1)} custom-call(bf16[16,192,128]{2,1,0:T(8,128)(2,1)S(1)} %all_to_all.18.recv_ref), custom_call_target="tpu_custom_call" | custom-call | tf_op jit(solution)/shard_map/cond/branch_1_fun/triangle/pallas_call | solution.py:239
  22.7 23.4 %all_to_all.19.recv_ref = bf16[32,96,128]{2,1,0:T(8,128)(2,1)S(1)} all-to-all(bf16[32,96,128]{2,1,0:T(8,128)(2,1)S(1)} %triangle.3), channel_id=1, replica_groups={{0,1,2,3,4,5,6,7,8,9,10,11,12,13,14,15,16,17,18,19,20,21,22,23,24,25,26..., dimensions={0} | all-to-all | bytes 1572864 | tf_op jit(solution)/shard_map/cond/branch_1_fun/all_to_all | solution.py:229
  46.1 1.7 %update.3 = f32[2048,128]{1,0:T(8,128)} custom-call(bf16[32,96,128]{2,1,0:T(8,128)(2,1)S(1)} %all_to_all.19.recv_ref, bf16[8,256,128]{2,1,0:T(8,128)(2,1)S(1)} %get-tuple-element.30.normed_ref, bf16[128,128]{1,0:T(8,128)(2,1)S(1)} %get-tuple-element.31.wg_ref, bf16[128,128]{1,0:T(8,128)(2,1)S(1)} %get-tuple-element.32.wo_ref), custom_call_target="tpu_custom_call" | custom-call | tf_op jit(solution)/shard_map/cond/branch_1_fun/update/pallas_call | solution.py:247
Async XLA Ops:
  0.0 2.6 %copy-start = (bf16[128,128]{1,0:T(8,128)(2,1)S(1)}, bf16[128,128]{1,0:T(8,128)(2,1)}, u32[]{:S(2)}) copy-start(bf16[128,128]{1,0:T(8,128)(2,1)} %param.12) | copy-start | bytes 98308
  0.0 2.6 %copy-start.1 = (bf16[128,128]{1,0:T(8,128)(2,1)S(1)}, bf16[128,128]{1,0:T(8,128)(2,1)}, u32[]{:S(2)}) copy-start(bf16[128,128]{1,0:T(8,128)(2,1)} %param.13) | copy-start | bytes 98308
